TPU v7x, 32 devices: a whole 2x2x4 slice. The times are simulated.
32 devices in a mesh: grp: 2 (over y), seq: 4 (over z), head: 2 (over x), sub: 2 (over core).
Axes of the slice: x: 2, y: 2, z: 4, core: 2. Of those that a mesh axis runs over, the one named last changes fastest.
Arguments:
- queries: bfloat16 [4096, 64, 128], P(('grp', 'seq', 'sub'), 'head'), parts along dimension 0, may hold values from -240 to 240
- keys: bfloat16 [4096, 8, 128], P(('grp', 'seq', 'sub'), 'head'), parts along dimension 0, may hold values from -240 to 240
- values: bfloat16 [4096, 8, 128], P(('grp', 'seq', 'sub'), 'head'), parts along dimension 0, may hold values from -6 to 6
- out_grad: bfloat16 [4096, 64, 128], P(('grp', 'seq', 'sub'), 'head'), parts along dimension 0, may hold values from -48 to 48
- feature_weights: bfloat16 [2, 64, 128, 128], P(None, 'head'), may hold values from -1.5 to 1.5
Outputs:
- query_grad: bfloat16 [4096, 64, 128], P(('grp', 'seq', 'sub'), 'head'), parts along dimension 0
- key_grad: bfloat16 [4096, 8, 128], P(('grp', 'seq', 'sub'), 'head'), parts along dimension 0
- value_grad: bfloat16 [4096, 8, 128], P(('grp', 'seq', 'sub'), 'head'), parts along dimension 0
- map_grads: float32 [256, 2, 64, 128], P(('grp', 'seq', 'sub'), None, 'head'), parts along dimension 0
There are 2 independent parts, one for each index of `grp`. A program takes and returns all parts, laid end to end along the dimension named above; an argument that names none is the same for every part. Nothing has to cross between parts.
All inputs are finite; a program needn't handle non-finite values.
Results may differ from a plain program's by a relative error of at most 0.014.
Values sent between devices are 32-bit elements; how exact they have to be, the bound alone decides.
A program may use at most 192 MiB of HBM per device.

v0:
```python
import jax
import jax.numpy as jnp
from jax import lax
from jax.sharding import PartitionSpec as P


def exclusive_sum(stack, reverse):
    if reverse:
        stack = jnp.flip(stack, 0)
    running = jnp.cumsum(stack, axis=0)
    shifted = jnp.concatenate([jnp.zeros_like(stack[:1]), running[:-1]], axis=0)
    if reverse:
        shifted = jnp.flip(shifted, 0)
    return shifted


def carry_states(matrix, vector, reverse):
    whole = lax.all_to_all(
        exclusive_sum(
            lax.all_to_all(matrix[None], ("seq", "sub"), split_axis=2, concat_axis=0, tiled=True),
            reverse,
        ),
        ("seq", "sub"),
        split_axis=0,
        concat_axis=2,
        tiled=True,
    )
    total = lax.all_to_all(
        exclusive_sum(
            lax.all_to_all(vector[None], ("seq", "sub"), split_axis=2, concat_axis=0, tiled=True),
            reverse,
        ),
        ("seq", "sub"),
        split_axis=0,
        concat_axis=2,
        tiled=True,
    )
    return (whole[0], total[0])


def lowp(form, left, right):
    return jnp.einsum(form, left, right, preferred_element_type=jnp.float32)


def exact(form, left, right):
    return jnp.einsum(form, left, right, precision=lax.Precision.HIGHEST)


def split_product(form, low_side, state):
    upper = state.astype(jnp.bfloat16)
    lower = (state - upper.astype(jnp.float32)).astype(jnp.bfloat16)
    return lowp(form, low_side, upper) + lowp(form, low_side, lower)


def feature_map(inputs, weight):
    return jax.nn.softmax(lowp("thd,hdf->thf", inputs, weight), axis=-1)


def logit_grad(feat, grad):
    return (feat * (grad - jnp.sum(feat * grad, axis=-1, keepdims=True))).astype(jnp.bfloat16)


def group_sum(rows, group_size):
    return jnp.sum(
        rows.reshape(rows.shape[0], rows.shape[1] // group_size, group_size, rows.shape[2]), axis=2
    )


def shards(queries, keys, values, out_grad, feature_weights):
    tokens = queries.shape[0]
    head_count = queries.shape[1]
    group_size = head_count // keys.shape[1]
    key_rows = jnp.repeat(keys, group_size, axis=1)
    value_rows = jnp.repeat(values, group_size, axis=1)
    query_map = feature_weights[0]
    key_map = feature_weights[1]
    query_feat = feature_map(queries, query_map)
    key_feat = feature_map(key_rows, key_map)
    query_low = query_feat.astype(jnp.bfloat16)
    key_low = key_feat.astype(jnp.bfloat16)
    kv_block = lowp("thf,thd->hfd", key_low, value_rows)
    z_block = jnp.sum(key_low.astype(jnp.float32), axis=0)
    state_kv, state_z = carry_states(kv_block, z_block, False)
    causal = jnp.arange(tokens)[:, None] >= jnp.arange(tokens)[None, :]
    masked = jnp.where(causal[None], lowp("thf,shf->hts", query_low, key_low), 0.0)
    weights = masked.astype(jnp.bfloat16)
    query_round = query_low.astype(jnp.float32)
    numerator = lowp("hts,shd->thd", weights, value_rows) + split_product(
        "thf,hfd->thd", query_low, state_kv
    )
    denominator = jnp.sum(masked, axis=2).T + exact("thf,hf->th", query_round, state_z)
    grad_wide = out_grad.astype(jnp.float32)
    numer_grad = (grad_wide / denominator[:, :, None]).astype(jnp.bfloat16)
    denom_grad = -jnp.sum(grad_wide * numerator, axis=2) / (denominator * denominator)
    back_block = lowp("thf,thd->hfd", query_low, numer_grad)
    back_z_block = exact("th,thf->hf", denom_grad, query_round)
    back_state, back_z = carry_states(back_block, back_z_block, True)
    score_grad = jnp.where(
        causal[None], lowp("thd,shd->hts", numer_grad, value_rows) + denom_grad.T[:, :, None], 0.0
    ).astype(jnp.bfloat16)
    query_feat_grad = (
        lowp("hts,shf->thf", score_grad, key_low)
        + split_product("thd,hfd->thf", numer_grad, state_kv)
        + denom_grad[:, :, None] * state_z[None]
    )
    key_feat_grad = (
        lowp("hts,thf->shf", score_grad, query_low)
        + split_product("shd,hfd->shf", value_rows, back_state)
        + back_z[None]
    )
    value_sum = lowp("hts,thd->shd", weights, numer_grad) + split_product(
        "shf,hfd->shd", key_low, back_state
    )
    query_logit_grad = logit_grad(query_feat, query_feat_grad)
    key_logit_grad = logit_grad(key_feat, key_feat_grad)
    query_grad = lowp("thf,hdf->thd", query_logit_grad, query_map).astype(jnp.bfloat16)
    key_grad = group_sum(lowp("thf,hdf->thd", key_logit_grad, key_map), group_size).astype(
        jnp.bfloat16
    )
    value_grad = group_sum(value_sum, group_size).astype(jnp.bfloat16)
    map_grads = lax.psum_scatter(
        jnp.stack(
            [
                lowp("thd,thf->dhf", queries, query_logit_grad),
                lowp("thd,thf->dhf", key_rows, key_logit_grad),
            ],
            axis=1,
        ),
        ("seq", "sub"),
        scatter_dimension=0,
        tiled=True,
    )
    return (query_grad, key_grad, value_grad, map_grads)


def solution(mesh):
    placed = (
        P(("grp", "seq", "sub"), "head", None),
        P(("grp", "seq", "sub"), "head", None),
        P(("grp", "seq", "sub"), "head", None),
        P(("grp", "seq", "sub"), "head", None),
        P(None, "head", None, None),
    )
    return jax.shard_map(
        shards,
        mesh=mesh,
        in_specs=placed,
        out_specs=(
            P(("grp", "seq", "sub"), "head", None),
            P(("grp", "seq", "sub"), "head", None),
            P(("grp", "seq", "sub"), "head", None),
            P(("grp", "seq", "sub"), None, "head", None),
        ),
        check_vma=False,
    )
```

profile of v0, /device:TPU:0, one launch (start us, length us, event | category | flops | bytes accessed | tf_op | source)
XLA Modules:
  0.0 384.3 jit_solution(18208326870646324169)
XLA Ops:
  11.3 3.9 %fusion.62 = (f32[256,32]{0,1:T(8,128)S(1)}, f32[256,32,128]{0,2,1:T(8,128)S(1)}) fusion(f32[32,128,256]{2,1,0:T(8,128)S(1)} %fusion.20), kind=kOutput, calls=%fused_computation.81 | output fusion | flops 2097279 | bytes 8421376 | tf_op jit(solution)/shard_map/sub | solution.py:56
  19.1 3.9 %fusion.61 = (f32[256,32]{0,1:T(8,128)S(1)}, f32[256,32,128]{0,2,1:T(8,128)S(1)}) fusion(f32[32,128,256]{2,1,0:T(8,128)S(1)} %fusion.29), kind=kOutput, calls=%fused_computation.80 | output fusion | flops 2097279 | bytes 8421376 | tf_op jit(solution)/shard_map/sub | solution.py:56
  23.1 2.9 convert_reduce_fusion
  28.4 6.3 %all-to-all-start = ((f32[8,1,512]{2,1,0:T(1,128)}), f32[8,1,512]{2,1,0:T(1,128)S(1)}, u32[]{:S(2)}, u32[]{:S(2)}) async-start(f32[8,1,512]{2,1,0:T(1,128)} %reshape.54), calls=%async_computation | async-start | bytes 32768 | tf_op jit(solution)/shard_map/all_to_all | solution.py:30
  40.4 4.5 %all-to-all-start.2 = ((f32[1,32,128,128]{3,1,0,2:T(8,128)}), f32[1,32,128,128]{3,1,0,2:T(8,128)}, u32[]{:S(2)}, u32[]{:S(2)}) async-start(f32[1,32,128,128]{3,1,0,2:T(8,128)} %copy.92), calls=%async_computation.2 | async-start | bytes 4194304 | tf_op jit(solution)/shard_map/all_to_all | solution.py:20
  46.7 47.4 %all-to-all-done.2 = f32[1,32,128,128]{3,1,0,2:T(8,128)} async-done(((f32[1,32,128,128]{3,1,0,2:T(8,128)}), f32[1,32,128,128]{3,1,0,2:T(8,128)}, u32[]{:S(2)}, u32[]{:S(2)}) %all-to-all-start.2) | async-done | bytes 2097184 | tf_op jit(solution)/shard_map/all_to_all | solution.py:20
  94.0 3.3 all-to-all-start.1
  97.4 2.9 fusion.15
  103.0 4.5 %all-to-all-start.3 = ((f32[8,32,16,128]{3,2,1,0:T(8,128)}), f32[8,32,16,128]{3,2,1,0:T(8,128)}, u32[]{:S(2)}, u32[]{:S(2)}) async-start(f32[8,32,16,128]{3,2,1,0:T(8,128)} %concatenate.13), calls=%async_computation.3 | async-start | bytes 4194304 | tf_op jit(solution)/shard_map/all_to_all | solution.py:18
  107.5 4.3 %copy.84 = bf16[256,32,128]{0,2,1:T(8,128)(2,1)} copy(bf16[256,32,128]{2,1,0:T(8,128)(2,1)} %param.8) | data formatting | bytes 4194304 | tf_op args[3]
  111.8 3.8 select_reduce_fusion
  117.7 2.9 fusion.26
  123.9 32.6 %all-to-all-done.3 = f32[8,32,16,128]{3,2,1,0:T(8,128)} async-done(((f32[8,32,16,128]{3,2,1,0:T(8,128)}), f32[8,32,16,128]{3,2,1,0:T(8,128)}, u32[]{:S(2)}, u32[]{:S(2)}) %all-to-all-start.3) | async-done | bytes 2097184 | tf_op jit(solution)/shard_map/all_to_all | solution.py:18
  156.5 3.2 copy.94
  159.7 2.9 copy.95
  162.6 3.1 fusion.48
  167.3 2.9 fusion.3
  173.6 3.3 all-to-all-start.6
  176.9 2.9 convolution_bitcast_fusion.1
  182.5 5.0 %all-to-all-start.4 = ((f32[1,32,128,128]{3,1,0,2:T(8,128)}), f32[1,32,128,128]{3,1,0,2:T(8,128)}, u32[]{:S(2)}, u32[]{:S(2)}) async-start(f32[1,32,128,128]{3,1,0,2:T(8,128)} %copy.110), calls=%async_computation.4 | async-start | bytes 4194304 | tf_op jit(solution)/shard_map/all_to_all | solution.py:20
  187.6 5.6 %select_convert_fusion = bf16[32,256,256]{1,2,0:T(8,128)(2,1)} fusion(f32[32,256]{1,0:T(8,128)S(1)} %bitcast_divide_fusion, pred[256,256]{0,1:T(8,128)(4,1)S(1)} %iota_compare_fusion, bf16[256,32,128]{2,0,1:T(8,128)(2,1)} %bitcast.178, bf16[256,32,128]{0,2,1:T(8,128)(2,1)} %copy.84, f32[256,32]{0,1:T(8,128)S(1)} %get-tuple-element.17), kind=kOutput, calls=%fused_computation.2 | convolution fusion | flops 546308096 | bytes 8519680 | tf_op jit(solution)/shard_map/thd,shd->hts/dot_general | solution.py:42
  195.0 41.7 %all-to-all-done.4 = f32[1,32,128,128]{3,1,0,2:T(8,128)} async-done(((f32[1,32,128,128]{3,1,0,2:T(8,128)}), f32[1,32,128,128]{3,1,0,2:T(8,128)}, u32[]{:S(2)}, u32[]{:S(2)}) %all-to-all-start.4) | async-done | bytes 2097184 | tf_op jit(solution)/shard_map/all_to_all | solution.py:20
  236.7 3.5 all-to-all-start.7
  240.2 4.1 %copy.175 = f32[1,32,8,16,128]{4,3,1,2,0:T(8,128)} copy(f32[1,32,8,16,128]{4,1,3,2,0:T(8,128)} %bitcast.33) | data formatting | bytes 4194304 | tf_op jit(solution)/shard_map/all_to_all | solution.py:20
  244.4 3.0 rev.14
  250.8 3.0 rev.15
  253.8 5.1 %all-to-all-start.5 = ((f32[8,32,16,128]{3,2,1,0:T(8,128)}), f32[8,32,16,128]{3,2,1,0:T(8,128)}, u32[]{:S(2)}, u32[]{:S(2)}) async-start(f32[8,32,16,128]{3,2,1,0:T(8,128)} %rev.15), calls=%async_computation.5 | async-start | bytes 4194304 | tf_op jit(solution)/shard_map/all_to_all | solution.py:18
  259.0 3.7 fusion.67
  273.4 3.5 fusion.68
  277.8 30.3 %all-to-all-done.5 = f32[8,32,16,128]{3,2,1,0:T(8,128)} async-done(((f32[8,32,16,128]{3,2,1,0:T(8,128)}), f32[8,32,16,128]{3,2,1,0:T(8,128)}, u32[]{:S(2)}, u32[]{:S(2)}) %all-to-all-start.5) | async-done | bytes 2097184 | tf_op jit(solution)/shard_map/all_to_all | solution.py:18
  322.2 5.8 %copy.122 = f32[128,2,32,128]{3,2,1,0:T(8,128)} copy(f32[128,2,32,128]{0,3,2,1:T(8,128)} %pad_maximum_fusion) | data formatting | bytes 8388608 | tf_op jit(solution)/shard_map/stack | solution.py:122
  340.6 36.4 %reduce-scatter.2.cloned.1.call-done = f32[16,2,32,128]{3,2,1,0:T(8,128)} async-done(((f32[128,2,32,128]{3,2,1,0:T(8,128)}), f32[16,2,32,128]{3,2,1,0:T(8,128)}) %reduce-scatter.2.cloned.1.call-update) | async-done | bytes 524304 | tf_op jit(solution)/shard_map/reduce_scatter | solution.py:121
  (137 shorter events, 76.9 us)
Async XLA Ops:
  11.3 3.9 %copy-start.31 = (bf16[256,4,128]{2,1,0:T(4,128)(2,1)S(1)}, bf16[256,4,128]{2,1,0:T(4,128)(2,1)}, u32[]{:S(2)}) copy-start(bf16[256,4,128]{2,1,0:T(4,128)(2,1)} %param.6) | copy-start | bytes 786436
  15.3 7.8 %copy-start.7 = (f32[256,32,128]{0,2,1:T(8,128)}, f32[256,32,128]{0,2,1:T(8,128)S(1)}, u32[]{:S(2)}) copy-start(f32[256,32,128]{0,2,1:T(8,128)S(1)} %get-tuple-element.23) | copy-start | bytes 12582916
  15.3 3.1 copy-start.26
  23.1 3.2 copy-start.5
  23.1 11.6 %copy-start.32 = (bf16[256,4,128]{2,1,0:T(4,128)(2,1)S(1)}, bf16[256,4,128]{2,1,0:T(4,128)(2,1)}, u32[]{:S(2)}) copy-start(bf16[256,4,128]{2,1,0:T(4,128)(2,1)} %param.7) | copy-start | bytes 786436
  28.4 12.0 %all-to-all-start = ((f32[8,1,512]{2,1,0:T(1,128)}), f32[8,1,512]{2,1,0:T(1,128)S(1)}, u32[]{:S(2)}, u32[]{:S(2)}) async-start(f32[8,1,512]{2,1,0:T(1,128)} %reshape.54), calls=%async_computation | async-start | bytes 32768 | tf_op jit(solution)/shard_map/all_to_all | solution.py:30
  40.4 53.6 %all-to-all-start.2 = ((f32[1,32,128,128]{3,1,0,2:T(8,128)}), f32[1,32,128,128]{3,1,0,2:T(8,128)}, u32[]{:S(2)}, u32[]{:S(2)}) async-start(f32[1,32,128,128]{3,1,0,2:T(8,128)} %copy.92), calls=%async_computation.2 | async-start | bytes 4194304 | tf_op jit(solution)/shard_map/all_to_all | solution.py:20
  94.0 8.9 %all-to-all-start.1 = ((f32[8,1,512]{2,1,0:T(1,128)}), f32[8,1,512]{2,1,0:T(1,128)S(1)}, u32[]{:S(2)}, u32[]{:S(2)}) async-start(f32[8,1,512]{2,1,0:T(1,128)} %reshape.56), calls=%async_computation.1 | async-start | bytes 32768 | tf_op jit(solution)/shard_map/all_to_all | solution.py:28
  103.0 53.6 %all-to-all-start.3 = ((f32[8,32,16,128]{3,2,1,0:T(8,128)}), f32[8,32,16,128]{3,2,1,0:T(8,128)}, u32[]{:S(2)}, u32[]{:S(2)}) async-start(f32[8,32,16,128]{3,2,1,0:T(8,128)} %concatenate.13), calls=%async_computation.3 | async-start | bytes 4194304 | tf_op jit(solution)/shard_map/all_to_all | solution.py:18
  111.8 5.9 %copy-start.10 = (bf16[256,4,8,128]{3,0,2,1:T(8,128)(2,1)S(1)}, bf16[256,4,8,128]{3,0,2,1:T(8,128)(2,1)}, u32[]{:S(2)}) copy-start(bf16[256,4,8,128]{3,0,2,1:T(8,128)(2,1)} %copy-done.9) | copy-start | bytes 6291460
  162.6 3.1 copy-start.1
  162.6 3.5 copy-start.17
  162.6 4.7 %copy-start.19 = (f32[32,256,128]{1,2,0:T(8,128)S(1)}, f32[32,256,128]{1,2,0:T(8,128)}, u32[]{:S(2)}) copy-start(f32[32,256,128]{1,2,0:T(8,128)} %fusion.26) | copy-start | bytes 12582916
  173.6 8.9 %all-to-all-start.6 = ((f32[8,1,512]{2,1,0:T(1,128)}), f32[8,1,512]{2,1,0:T(1,128)S(1)}, u32[]{:S(2)}, u32[]{:S(2)}) async-start(f32[8,1,512]{2,1,0:T(1,128)} %reshape.58), calls=%async_computation.6 | async-start | bytes 32768 | tf_op jit(solution)/shard_map/all_to_all | solution.py:30
  182.5 54.1 %all-to-all-start.4 = ((f32[1,32,128,128]{3,1,0,2:T(8,128)}), f32[1,32,128,128]{3,1,0,2:T(8,128)}, u32[]{:S(2)}, u32[]{:S(2)}) async-start(f32[1,32,128,128]{3,1,0,2:T(8,128)} %copy.110), calls=%async_computation.4 | async-start | bytes 4194304 | tf_op jit(solution)/shard_map/all_to_all | solution.py:20
  236.7 17.2 %all-to-all-start.7 = ((f32[8,1,512]{2,1,0:T(1,128)}), f32[8,1,512]{2,1,0:T(1,128)S(1)}, u32[]{:S(2)}, u32[]{:S(2)}) async-start(f32[8,1,512]{2,1,0:T(1,128)} %reshape.60), calls=%async_computation.7 | async-start | bytes 32768 | tf_op jit(solution)/shard_map/all_to_all | solution.py:28
  253.8 54.2 %all-to-all-start.5 = ((f32[8,32,16,128]{3,2,1,0:T(8,128)}), f32[8,32,16,128]{3,2,1,0:T(8,128)}, u32[]{:S(2)}, u32[]{:S(2)}) async-start(f32[8,32,16,128]{3,2,1,0:T(8,128)} %rev.15), calls=%async_computation.5 | async-start | bytes 4194304 | tf_op jit(solution)/shard_map/all_to_all | solution.py:18
  258.9 118.1 %reduce-scatter.2.cloned.1.call-start = ((), (), s32[]{:S(2)}) async-start(), calls=%async_computation.9 | async-start | bytes 4718592 | tf_op jit(solution)/shard_map/reduce_scatter | solution.py:121
  259.0 3.7 copy-start.18
  259.0 4.1 %copy-start.23 = (bf16[256,32,128]{0,2,1:T(8,128)(2,1)S(1)}, bf16[256,32,128]{0,2,1:T(8,128)(2,1)}, u32[]{:S(2)}) copy-start(bf16[256,32,128]{0,2,1:T(8,128)(2,1)} %copy.84) | copy-start | bytes 6291460
  263.0 2.2 copy-start.8
  269.1 2.7 copy-start.16
  269.1 2.7 copy-start.2
  269.1 4.3 %copy-start.20 = (bf16[32,256,256]{1,2,0:T(8,128)(2,1)S(1)}, bf16[32,256,256]{1,2,0:T(8,128)(2,1)}, u32[]{:S(2)}) copy-start(bf16[32,256,256]{1,2,0:T(8,128)(2,1)} %select_convert_fusion) | copy-start | bytes 12582916
  308.1 2.2 copy-start.11
  310.3 2.7 copy-start.6
  310.3 4.0 %copy-start.30 = (f32[32,128,256]{2,1,0:T(8,128)S(1)}, f32[32,128,256]{2,1,0:T(8,128)}, u32[]{:S(2)}) copy-start(f32[32,128,256]{2,1,0:T(8,128)} %fusion.68) | copy-start | bytes 12582916
  317.6 2.3 copy-start.25
  327.9 5.5 %copy-start.29 = (bf16[32,256,256]{1,2,0:T(8,128)(2,1)S(1)}, bf16[32,256,256]{1,2,0:T(8,128)(2,1)}, u32[]{:S(2)}) copy-start(bf16[32,256,256]{1,2,0:T(8,128)(2,1)} %copy-done.28) | copy-start | bytes 12582916
  330.7 2.7 copy-start.24
  333.4 2.2 copy-start.27
  335.6 2.3 copy-start.13
  (10 other events, 16.2 us)
Sparse Core Ops, SparseCore 0:
  328.1 48.9 reduce-scatter.1
where the time goes:
time: 392 us; the launch traced here: 384 us
  waiting for transfers between devices  190 us (48%)
  local copies, waits for them, and re-layouts  66 us (17%)
  matrix products  52.7 us (13%)
  starting transfers between devices  35.6 us (9%)
  other arithmetic  24.8 us (6%)
  between operations  15.1 us (4%)
    all_to_all x2, waiting for transfers between devices, carry_states(): lax.all_to_all(matrix[None], ('seq', 'sub'), split_axis=2, concat_axis=0,...  89.1 us
    all_to_all x2, waiting for transfers between devices, carry_states(): lax.all_to_all(exclusive_sum(lax.all_to_all(matrix[None], ('seq', 'sub'),...  62.9 us
    dot_general x22, matrix products, lowp(): return jnp.einsum(form, left, right, preferred_element_type=jnp.float32)  48.5 us
    reduce_scatter x1, waiting for transfers between devices, shards(): lax.psum_scatter(jnp.stack([lowp('thd,thf->dhf', queries, query_logit_gra...  36.4 us
    unnamed x83, local copies, waits for them, and re-layouts  32.2 us
    all_to_all x2, starting transfers between devices, carry_states(): lax.all_to_all(vector[None], ('seq', 'sub'), split_axis=2, concat_axis=0,...  9.67 us
    all_to_all x2, starting transfers between devices, carry_states(): lax.all_to_all(exclusive_sum(lax.all_to_all(matrix[None], ('seq', 'sub'),...  9.57 us
    all_to_all x2, starting transfers between devices, carry_states(): lax.all_to_all(matrix[None], ('seq', 'sub'), split_axis=2, concat_axis=0,...  9.43 us
  transfers between devices with their start and end apart: 9, of which 8 were waited for; matrix products, arithmetic and copies ran while one was open for 20% of the time, Pallas kernels for 0%

commit v1 on v0

v1 whole, which is shorter than its diff:
```python
import functools

import jax
import jax.numpy as jnp
from jax import lax
from jax.experimental import pallas as pl
from jax.experimental.pallas import tpu as pltpu
from jax.sharding import PartitionSpec as P

F32 = jnp.float32
BF16 = jnp.bfloat16


def dot(left, right, left_dim, right_dim):
    return lax.dot_general(
        left, right, (((left_dim,), (right_dim,)), ((), ())), preferred_element_type=F32
    )


def softmax(logits):
    grown = jnp.exp(logits - jnp.max(logits, axis=1, keepdims=True))
    return grown * (1.0 / jnp.sum(grown, axis=1, keepdims=True))


def logit_grad(low, grad):
    feat = low.astype(F32)
    return (feat * (grad - jnp.sum(feat * grad, axis=1, keepdims=True))).astype(BF16)


def kernel(
    blocks, subs, group_size,
    q_ref, k_ref, v_ref, og_ref, w_ref,
    qg_ref, kg_ref, vg_ref, mg_ref,
    ql_ref, kl_ref, ng_ref, dg_ref, wt_ref,
    fwd_in, fwd_out, bwd_in, bwd_out, k_acc, v_acc,
    fwd_send, fwd_recv, bwd_send, bwd_recv,
):
    heads, tokens, width = q_ref.shape
    feats = w_ref.shape[3]
    me = lax.axis_index("seq") * subs + lax.axis_index("sub")
    first = me == 0
    last = me == blocks - 1
    before = jnp.maximum(me - 1, 0)
    after = jnp.minimum(me + 1, blocks - 1)

    def place(block):
        return {"seq": block // subs, "sub": block % subs}

    def fwd_copy(h):
        return pltpu.make_async_remote_copy(
            src_ref=fwd_out.at[h], dst_ref=fwd_in.at[h],
            send_sem=fwd_send.at[h], recv_sem=fwd_recv.at[h],
            device_id=place(after), device_id_type=pl.DeviceIdType.MESH,
        )

    def bwd_copy(h):
        return pltpu.make_async_remote_copy(
            src_ref=bwd_out.at[h], dst_ref=bwd_in.at[h],
            send_sem=bwd_send.at[h], recv_sem=bwd_recv.at[h],
            device_id=place(before), device_id_type=pl.DeviceIdType.MESH,
        )

    barrier = pltpu.get_barrier_semaphore()

    @pl.when(me > 0)
    def _():
        pl.semaphore_signal(
            barrier, inc=1, device_id=place(before), device_id_type=pl.DeviceIdType.MESH
        )

    @pl.when(me < blocks - 1)
    def _():
        pl.semaphore_signal(
            barrier, inc=1, device_id=place(after), device_id_type=pl.DeviceIdType.MESH
        )

    inner = jnp.logical_and(me > 0, me < blocks - 1)

    @pl.when(inner)
    def _():
        pl.semaphore_wait(barrier, 2)

    @pl.when(jnp.logical_not(inner))
    def _():
        pl.semaphore_wait(barrier, 1)

    @pl.when(first)
    def _():
        fwd_in[...] = jnp.zeros_like(fwd_in)

    @pl.when(last)
    def _():
        bwd_in[...] = jnp.zeros_like(bwd_in)

    def features(h, carry):
        g = h // group_size
        ql_ref[h] = softmax(dot(q_ref[h], w_ref[0, h], 1, 0)).astype(BF16)
        key_low = softmax(dot(k_ref[g], w_ref[1, h], 1, 0)).astype(BF16)
        kl_ref[h] = key_low
        own = dot(v_ref[g], key_low, 0, 0)
        own_z = jnp.sum(key_low.astype(F32), axis=0, keepdims=True)

        @pl.when(me > 0)
        def _():
            fwd_copy(h).wait_recv()

        @pl.when(me < blocks - 1)
        def _():
            fwd_out[h, 0:width] = fwd_in[h, 0:width] + own
            fwd_out[h, width:width + 8] = fwd_in[h, width:width + 8] + own_z
            fwd_copy(h).start()

        return carry

    lax.fori_loop(0, heads, features, 0)

    def causal():
        rows = lax.broadcasted_iota(jnp.int32, (tokens, tokens), 0)
        return rows >= lax.broadcasted_iota(jnp.int32, (tokens, tokens), 1)

    def forward(h, carry):
        g = h // group_size
        query_low = ql_ref[h]
        masked = jnp.where(causal(), dot(query_low, kl_ref[h], 1, 1), 0.0)
        weights = masked.astype(BF16)
        wt_ref[h] = weights
        numerator = dot(weights, v_ref[g], 1, 0) + dot(
            query_low, fwd_in[h, 0:width].astype(BF16), 1, 1
        )
        query_round = query_low.astype(F32)
        denominator = jnp.sum(masked, axis=1, keepdims=True) + jnp.sum(
            query_round * fwd_in[h, width:width + 1], axis=1, keepdims=True
        )
        grad = og_ref[h].astype(F32)
        numer_grad = (grad * (1.0 / denominator)).astype(BF16)
        denom_grad = -jnp.sum(grad * numerator, axis=1, keepdims=True) / (
            denominator * denominator
        )
        ng_ref[h] = numer_grad
        dg_ref[h] = denom_grad
        own = dot(numer_grad, query_low, 0, 0)
        own_z = jnp.sum(query_round * denom_grad, axis=0, keepdims=True)

        @pl.when(me < blocks - 1)
        def _():
            bwd_copy(h).wait_recv()

        @pl.when(me > 0)
        def _():
            bwd_out[h, 0:width] = bwd_in[h, 0:width] + own
            bwd_out[h, width:width + 8] = bwd_in[h, width:width + 8] + own_z
            bwd_copy(h).start()

        return carry

    lax.fori_loop(0, heads, forward, 0)

    def backward(h, carry):
        g = h // group_size
        query_low = ql_ref[h]
        key_low = kl_ref[h]
        numer_grad = ng_ref[h]
        denom_grad = dg_ref[h]
        value_rows = v_ref[g]
        score_grad = jnp.where(
            causal(), dot(numer_grad, value_rows, 1, 1) + denom_grad, 0.0
        ).astype(BF16)
        query_feat_grad = (
            dot(score_grad, key_low, 1, 0)
            + dot(numer_grad, fwd_in[h, 0:width].astype(BF16), 1, 0)
            + denom_grad * fwd_in[h, width:width + 1]
        )
        query_logit_grad = logit_grad(query_low, query_feat_grad)
        qg_ref[h] = dot(query_logit_grad, w_ref[0, h], 1, 1).astype(BF16)
        parts = mg_ref.shape[0]
        mg_ref[:, 0, h] = dot(q_ref[h], query_logit_grad, 0, 0).reshape(
            parts, width // parts, feats
        )
        back = bwd_in[h, 0:width].astype(BF16)
        key_feat_grad = (
            dot(score_grad, query_low, 0, 0)
            + dot(value_rows, back, 1, 0)
            + bwd_in[h, width:width + 1]
        )
        key_logit_grad = logit_grad(key_low, key_feat_grad)
        mg_ref[:, 1, h] = dot(k_ref[g], key_logit_grad, 0, 0).reshape(
            parts, width // parts, feats
        )
        key_term = dot(key_logit_grad, w_ref[1, h], 1, 1)
        value_term = dot(wt_ref[h], numer_grad, 0, 0) + dot(key_low, back, 1, 1)
        fresh = h % group_size == 0

        @pl.when(fresh)
        def _():
            k_acc[...] = key_term
            v_acc[...] = value_term

        @pl.when(jnp.logical_not(fresh))
        def _():
            k_acc[...] += key_term
            v_acc[...] += value_term

        @pl.when(h % group_size == group_size - 1)
        def _():
            kg_ref[g] = k_acc[...].astype(BF16)
            vg_ref[g] = v_acc[...].astype(BF16)

        return carry

    lax.fori_loop(0, heads, backward, 0)

    def drain(h, carry):
        @pl.when(me < blocks - 1)
        def _():
            fwd_copy(h).wait_send()

        @pl.when(me > 0)
        def _():
            bwd_copy(h).wait_send()

        return carry

    lax.fori_loop(0, heads, drain, 0)


def shards(blocks, subs, queries, keys, values, out_grad, feature_weights):
    tokens, heads, width = queries.shape
    groups = keys.shape[1]
    feats = feature_weights.shape[3]
    rows = width // blocks
    vmem = pl.BlockSpec(memory_space=pltpu.VMEM)
    slot = pltpu.VMEM((heads, width + 8, feats), F32)
    query_grad, key_grad, value_grad, maps = pl.pallas_call(
        functools.partial(kernel, blocks, subs, heads // groups),
        out_shape=(
            jax.ShapeDtypeStruct((heads, tokens, width), BF16),
            jax.ShapeDtypeStruct((groups, tokens, width), BF16),
            jax.ShapeDtypeStruct((groups, tokens, width), BF16),
            jax.ShapeDtypeStruct((blocks, 2, heads, rows, feats), F32),
        ),
        in_specs=[vmem] * 5,
        out_specs=(vmem,) * 4,
        scratch_shapes=[
            pltpu.VMEM((heads, tokens, feats), BF16),
            pltpu.VMEM((heads, tokens, feats), BF16),
            pltpu.VMEM((heads, tokens, width), BF16),
            pltpu.VMEM((heads, tokens, 1), F32),
            pltpu.VMEM((heads, tokens, tokens), BF16),
            slot, slot, slot, slot,
            pltpu.VMEM((tokens, width), F32),
            pltpu.VMEM((tokens, width), F32),
            pltpu.SemaphoreType.DMA((heads,)),
            pltpu.SemaphoreType.DMA((heads,)),
            pltpu.SemaphoreType.DMA((heads,)),
            pltpu.SemaphoreType.DMA((heads,)),
        ],
        compiler_params=pltpu.CompilerParams(
            collective_id=0, has_side_effects=True, vmem_limit_bytes=56 * 1024 * 1024
        ),
    )(
        queries.transpose(1, 0, 2),
        keys.transpose(1, 0, 2),
        values.transpose(1, 0, 2),
        out_grad.transpose(1, 0, 2),
        feature_weights,
    )
    summed = lax.psum_scatter(maps, ("seq", "sub"), scatter_dimension=0, tiled=True)
    return (
        query_grad.transpose(1, 0, 2),
        key_grad.transpose(1, 0, 2),
        value_grad.transpose(1, 0, 2),
        summed[0].transpose(2, 0, 1, 3),
    )


def solution(mesh):
    subs = mesh.shape["sub"]
    blocks = mesh.shape["seq"] * subs
    rows = P(("grp", "seq", "sub"), "head", None)
    return jax.shard_map(
        functools.partial(shards, blocks, subs),
        mesh=mesh,
        in_specs=(rows, rows, rows, rows, P(None, "head", None, None)),
        out_specs=(rows, rows, rows, P(("grp", "seq", "sub"), None, "head", None)),
        check_vma=False,
    )
```

time: 392 us -> 186 us (0.47); the launches traced: 384 us -> 186 us
  waiting for transfers between devices: 190 us -> 42.3 us
  Pallas kernels: 0 us -> 114 us
  matrix products: 52.7 us -> 0 us
  local copies, waits for them, and re-layouts: 66 us -> 15.8 us
  starting transfers between devices: 35.6 us -> 0.04 us
  other arithmetic: 24.8 us -> 0 us
    all_to_all x8 -> x0, waiting for transfers between devices: 154 us -> none  [the longest x2 89.1 us: carry_states(): lax.all_to_all(matrix[None], ('seq', 'sub'), split_axis=2, concat_axis=0,...]
    pallas_call x0 -> x1, Pallas kernels: none -> 114 us  [shards(): pl.pallas_call(functools.partial(kernel, blocks, subs, heads // groups),...]
    dot_general x24 -> x0, matrix products: 52.7 us -> none  [the longest x22 48.5 us: lowp(): return jnp.einsum(form, left, right, preferred_element_type=jnp.float32)]
    all_to_all x8 -> x0, starting transfers between devices: 35.5 us -> none  [the longest x2 9.67 us: carry_states(): lax.all_to_all(vector[None], ('seq', 'sub'), split_axis=2, concat_axis=0,...]
    unnamed x83 -> x10, local copies, waits for them, and re-layouts: 32.2 us -> 8.06 us
    all_to_all x3 -> x0, local copies, waits for them, and re-layouts: 9.31 us -> none  [the longest x2 5.17 us: carry_states(): lax.all_to_all(exclusive_sum(lax.all_to_all(matrix[None], ('seq', 'sub'),...]
    sub x2 -> x0, other arithmetic: 7.85 us -> none  [feature_map(): return jax.nn.softmax(lowp('thd,hdf->thf', inputs, weight), axis=-1)]
    transpose x0 -> x2, local copies, waits for them, and re-layouts: none -> 7.76 us  [the longest x1 5.88 us: shards(): out_grad.transpose(1, 0, 2)]
  transfers between devices with their start and end apart: 9 -> 1, of which waited for: 8 -> 1; matrix products, arithmetic and copies ran while one was open for 20% -> 2% of each run, Pallas kernels for 0% -> 0%
where the time goes in v1:
time: 186 us
  Pallas kernels  114 us (61%)
  waiting for transfers between devices  42.3 us (23%)
  local copies, waits for them, and re-layouts  15.8 us (8%)
  between operations  14 us (8%)
    pallas_call x1, Pallas kernels, shards(): pl.pallas_call(functools.partial(kernel, blocks, subs, heads // groups),...  114 us
    reduce_scatter x1, waiting for transfers between devices, shards(): lax.psum_scatter(maps, ('seq', 'sub'), scatter_dimension=0, tiled=True)  42.3 us
    unnamed x10, local copies, waits for them, and re-layouts  8.06 us
    transpose x1, local copies, waits for them, and re-layouts, shards(): out_grad.transpose(1, 0, 2)  5.88 us
  transfers between devices with their start and end apart: 1, of which 1 were waited for; matrix products, arithmetic and copies ran while one was open for 2% of the time, Pallas kernels for 0%

profile of v1, /device:TPU:0, one launch (start us, length us, event | category | flops | bytes accessed | tf_op | source)
XLA Modules:
  0.0 185.9 jit_solution(1279541463037898412)
XLA Ops:
  7.2 0.0 reduce-scatter.2.cloned.1.call-start
  7.2 1.9 %copy_bitcast_fusion.2 = (bf16[4,256,128]{2,1,0:T(8,128)(2,1)}, bf16[4,256,128]{2,1,0:T(8,128)(2,1)}) fusion(bf16[256,4,128]{2,1,0:T(4,128)(2,1)} %param.7, bf16[256,4,128]{2,1,0:T(4,128)(2,1)} %param.6), kind=kLoop, calls=%fused_computation.2 | loop fusion | bytes 1048576 | tf_op jit(solution)/shard_map/transpose | solution.py:263
  9.1 5.9 %copy_bitcast_fusion = (bf16[32,256,128]{2,1,0:T(8,128)(2,1)}, bf16[32,256,128]{2,1,0:T(8,128)(2,1)}) fusion(bf16[256,32,128]{2,1,0:T(8,128)(2,1)} %param.8, bf16[256,32,128]{2,1,0:T(8,128)(2,1)} %param.5), kind=kLoop, calls=%fused_computation | loop fusion | bytes 8388608 | tf_op jit(solution)/shard_map/transpose | solution.py:264
  15.0 113.7 %shard_map.84 = (bf16[32,256,128]{2,1,0:T(8,128)(2,1)}, bf16[4,256,128]{2,1,0:T(8,128)(2,1)}, bf16[4,256,128]{2,1,0:T(8,128)(2,1)}, f32[8,2,32,16,128]{4,3,2,1,0:T(8,128)}) custom-call(bf16[32,256,128]{2,1,0:T(8,128)(2,1)} %get-tuple-element.17.q_ref, bf16[4,256,128]{2,1,0:T(8,128)(2,1)} %get-tuple-element.19.k_ref, ...), custom_call_target="tpu_custom_call" | custom-call | tf_op jit(solution)/shard_map/pallas_call | solution.py:233
  128.7 0.0 copy-start
  128.7 0.0 reduce-scatter.2.cloned.1.call-update
  128.7 1.6 copy-done
  130.3 0.0 copy-start.2
  130.3 0.0 copy-start.1
  130.3 2.7 %copy.13 = bf16[256,32,128]{2,1,0:T(8,128)(2,1)} copy(bf16[256,32,128]{2,0,1:T(8,128)(2,1)S(1)} %bitcast.14) | data formatting | bytes 4194304
  132.9 0.0 copy-done.2
  132.9 0.9 copy.14
  133.8 0.0 copy-done.1
  133.8 0.9 copy.15
  134.7 42.3 %reduce-scatter.2.cloned.1.call-done = f32[1,2,32,16,128]{4,3,2,1,0:T(8,128)} async-done(((f32[8,2,32,16,128]{4,3,2,1,0:T(8,128)}), f32[1,2,32,16,128]{4,3,2,1,0:T(8,128)}) %reduce-scatter.2.cloned.1.call-update) | async-done | bytes 524304 | tf_op jit(solution)/shard_map/reduce_scatter | solution.py:267
  177.1 2.0 %copy.16 = f32[16,2,32,128]{3,2,1,0:T(8,128)} copy(f32[16,2,32,128]{3,0,2,1:T(8,128)} %bitcast.15) | data formatting | bytes 1048576
Async XLA Ops:
  7.2 169.9 %reduce-scatter.2.cloned.1.call-start = ((), (), s32[]{:S(2)}) async-start(), calls=%async_computation.1 | async-start | bytes 4718592 | tf_op jit(solution)/shard_map/reduce_scatter | solution.py:267
  128.7 1.6 copy-start
  130.3 2.7 %copy-start.2 = (bf16[4,256,128]{2,1,0:T(8,128)(2,1)S(1)}, bf16[4,256,128]{2,1,0:T(8,128)(2,1)}, u32[]{:S(2)}) copy-start(bf16[4,256,128]{2,1,0:T(8,128)(2,1)} %get-tuple-element.9) | copy-start | bytes 786436
  130.3 3.6 %copy-start.1 = (bf16[4,256,128]{2,1,0:T(8,128)(2,1)S(1)}, bf16[4,256,128]{2,1,0:T(8,128)(2,1)}, u32[]{:S(2)}) copy-start(bf16[4,256,128]{2,1,0:T(8,128)(2,1)} %get-tuple-element.10) | copy-start | bytes 786436
Sparse Core Ops, SparseCore 0:
  128.8 48.2 reduce-scatter.1

commit v2 on v1

v2 whole, which is shorter than its diff:
```python
import functools

import jax
import jax.numpy as jnp
from jax import lax
from jax.experimental import pallas as pl
from jax.experimental.pallas import tpu as pltpu
from jax.sharding import PartitionSpec as P

F32 = jnp.float32
BF16 = jnp.bfloat16
LAG = 2


def dot(left, right, left_dim, right_dim):
    return lax.dot_general(
        left, right, (((left_dim,), (right_dim,)), ((), ())), preferred_element_type=F32
    )


def softmax(logits):
    grown = jnp.exp(logits - jnp.max(logits, axis=1, keepdims=True))
    return grown * (1.0 / jnp.sum(grown, axis=1, keepdims=True))


def logit_grad(low, grad):
    feat = low.astype(F32)
    return (feat * (grad - jnp.sum(feat * grad, axis=1, keepdims=True))).astype(BF16)


def kernel(
    chips, subs, group_size, batch,
    q_ref, k_ref, v_ref, og_ref, w_ref,
    qg_ref, kg_ref, vg_ref, mg_ref,
    ql_ref, kl_ref, kf_ref,
    fwd_in, fwd_out, bwd_in, bwd_out, k_acc, v_acc,
    map_own, map_got, map_sum, map_far,
    fwd_send, fwd_recv, bwd_send, bwd_recv,
    pair_send, pair_recv, far_send, far_recv,
):
    heads, tokens, width = q_ref.shape
    feats = w_ref.shape[3]
    blocks = chips * subs
    chip = lax.axis_index("seq")
    core = lax.axis_index("sub")
    me = chip * subs + core
    before = jnp.maximum(me - 1, 0)
    after = jnp.minimum(me + 1, blocks - 1)
    batches = heads // batch

    def place(block):
        return {"seq": block // subs, "sub": block % subs}

    def send(src, dst, send_sem, recv_sem, target):
        return pltpu.make_async_remote_copy(
            src_ref=src, dst_ref=dst, send_sem=send_sem, recv_sem=recv_sem,
            device_id=target, device_id_type=pl.DeviceIdType.MESH,
        )

    def fwd_copy(h):
        return send(
            fwd_out.at[h], fwd_in.at[h], fwd_send.at[h], fwd_recv.at[h], place(after)
        )

    def bwd_copy(h):
        return send(
            bwd_out.at[h], bwd_in.at[h], bwd_send.at[h], bwd_recv.at[h], place(before)
        )

    def pair_copy(side, n):
        return send(
            map_own.at[side, n, 1 - core], map_got.at[side, n],
            pair_send.at[side, n], pair_recv.at[side, n],
            {"seq": chip, "sub": 1 - core},
        )

    def far_copy(side, n, hop):
        to = (chip + hop) % chips
        return send(
            map_sum.at[side, n, to], map_far.at[hop - 1, side, n],
            far_send.at[hop - 1, side, n], far_recv.at[hop - 1, side, n],
            {"seq": to, "sub": core},
        )

    barrier = pltpu.get_barrier_semaphore()
    for step in range(1, blocks):
        pl.semaphore_signal(
            barrier, inc=1, device_id=place((me + step) % blocks),
            device_id_type=pl.DeviceIdType.MESH,
        )
    pl.semaphore_wait(barrier, blocks - 1)

    @pl.when(me == 0)
    def _():
        fwd_in[...] = jnp.zeros_like(fwd_in)

    @pl.when(me == blocks - 1)
    def _():
        bwd_in[...] = jnp.zeros_like(bwd_in)

    fwd_lag = jnp.minimum(LAG * me, heads // 2)
    bwd_lag = jnp.minimum(LAG * (blocks - 1 - me), heads // 2)

    def fwd_step(h):
        @pl.when(me > 0)
        def _():
            fwd_copy(h).wait_recv()

        @pl.when(me < blocks - 1)
        def _():
            fwd_out[h] += fwd_in[h]
            fwd_copy(h).start()

    def bwd_step(h):
        @pl.when(me < blocks - 1)
        def _():
            bwd_copy(h).wait_recv()

        @pl.when(me > 0)
        def _():
            bwd_out[h] += bwd_in[h]
            bwd_copy(h).start()

    def put_map(side, h, product):
        n = h // batch
        rows = product.reshape(chips, subs, width // blocks, feats)
        for c in range(subs):
            map_own[side, n, c, :, h % batch] = rows[:, c]

        @pl.when(h % batch == batch - 1)
        def _():
            pair_copy(side, n).start()

    def spread_map(side, n):
        pair_copy(side, n).wait_recv()
        map_sum[side, n] = map_own[side, n, core] + map_got[side, n]
        for hop in range(1, chips):
            far_copy(side, n, hop).start()

    def features(h, carry):
        g = h // group_size
        ql_ref[h] = softmax(dot(q_ref[h], w_ref[0, h], 1, 0)).astype(BF16)
        key_low = softmax(dot(k_ref[g], w_ref[1, h], 1, 0)).astype(BF16)
        kl_ref[h] = key_low
        fwd_out[h, 0:width] = dot(v_ref[g], key_low, 0, 0)
        fwd_out[h, width:width + 8] = jnp.broadcast_to(
            jnp.sum(key_low.astype(F32), axis=0, keepdims=True), (8, feats)
        )

        @pl.when(h >= fwd_lag)
        def _():
            fwd_step(h - fwd_lag)

        return carry

    lax.fori_loop(0, heads, features, 0)

    def causal():
        rows = lax.broadcasted_iota(jnp.int32, (tokens, tokens), 0)
        return rows >= lax.broadcasted_iota(jnp.int32, (tokens, tokens), 1)

    def queries_side(h, carry):
        @pl.when(h < fwd_lag)
        def _():
            fwd_step(heads - fwd_lag + h)

        g = h // group_size
        query_low = ql_ref[h]
        key_low = kl_ref[h]
        value_rows = v_ref[g]
        state = fwd_in[h, 0:width].astype(BF16)
        state_z = fwd_in[h, width:width + 1]
        masked = jnp.where(causal(), dot(query_low, key_low, 1, 1), 0.0)
        weights = masked.astype(BF16)
        numerator = dot(weights, value_rows, 1, 0) + dot(query_low, state, 1, 1)
        query_round = query_low.astype(F32)
        denominator = jnp.sum(masked, axis=1, keepdims=True) + jnp.sum(
            query_round * state_z, axis=1, keepdims=True
        )
        grad = og_ref[h].astype(F32)
        numer_grad = (grad * (1.0 / denominator)).astype(BF16)
        denom_grad = -jnp.sum(grad * numerator, axis=1, keepdims=True) / (
            denominator * denominator
        )
        bwd_out[h, 0:width] = dot(numer_grad, query_low, 0, 0)
        bwd_out[h, width:width + 8] = jnp.broadcast_to(
            jnp.sum(query_round * denom_grad, axis=0, keepdims=True), (8, feats)
        )

        @pl.when(h >= bwd_lag)
        def _():
            bwd_step(h - bwd_lag)

        score_grad = jnp.where(
            causal(), dot(numer_grad, value_rows, 1, 1) + denom_grad, 0.0
        ).astype(BF16)
        query_feat_grad = (
            dot(score_grad, key_low, 1, 0)
            + dot(numer_grad, state, 1, 0)
            + denom_grad * state_z
        )
        query_logit_grad = logit_grad(query_low, query_feat_grad)
        qg_ref[h] = dot(query_logit_grad, w_ref[0, h], 1, 1).astype(BF16)
        put_map(0, h, dot(q_ref[h], query_logit_grad, 0, 0))
        kf_ref[h] = dot(score_grad, query_low, 0, 0)
        value_term = dot(weights, numer_grad, 0, 0)
        fresh = h % group_size == 0

        @pl.when(fresh)
        def _():
            v_acc[g] = value_term

        @pl.when(jnp.logical_not(fresh))
        def _():
            v_acc[g] += value_term

        @pl.when(jnp.logical_and(h % batch == 1, h >= batch))
        def _():
            spread_map(0, h // batch - 1)

        return carry

    lax.fori_loop(0, heads, queries_side, 0)

    def keys_side(h, carry):
        @pl.when(h < bwd_lag)
        def _():
            bwd_step(heads - bwd_lag + h)

        @pl.when(h == 1)
        def _():
            spread_map(0, batches - 1)

        g = h // group_size
        key_low = kl_ref[h]
        back = bwd_in[h, 0:width].astype(BF16)
        key_feat_grad = (
            kf_ref[h] + dot(v_ref[g], back, 1, 0) + bwd_in[h, width:width + 1]
        )
        key_logit_grad = logit_grad(key_low, key_feat_grad)
        put_map(1, h, dot(k_ref[g], key_logit_grad, 0, 0))
        key_term = dot(key_logit_grad, w_ref[1, h], 1, 1)
        v_acc[g] += dot(key_low, back, 1, 1)
        fresh = h % group_size == 0

        @pl.when(fresh)
        def _():
            k_acc[...] = key_term

        @pl.when(jnp.logical_not(fresh))
        def _():
            k_acc[...] += key_term

        @pl.when(h % group_size == group_size - 1)
        def _():
            kg_ref[g] = k_acc[...].astype(BF16)
            vg_ref[g] = v_acc[g].astype(BF16)

        @pl.when(jnp.logical_and(h % batch == 1, h >= batch))
        def _():
            spread_map(1, h // batch - 1)

        return carry

    lax.fori_loop(0, heads, keys_side, 0)
    spread_map(1, batches - 1)

    for side in range(2):
        def finish(n, carry):
            total = map_sum[side, n, chip]
            for hop in range(1, chips):
                far_copy(side, n, hop).wait_recv()
                total += map_far[hop - 1, side, n]
            mg_ref[side, n] = total
            pair_copy(side, n).wait_send()
            for hop in range(1, chips):
                far_copy(side, n, hop).wait_send()
            return carry

        lax.fori_loop(0, batches, finish, 0)

    def drain(h, carry):
        @pl.when(me < blocks - 1)
        def _():
            fwd_copy(h).wait_send()

        @pl.when(me > 0)
        def _():
            bwd_copy(h).wait_send()

        return carry

    lax.fori_loop(0, heads, drain, 0)


def shards(chips, subs, queries, keys, values, out_grad, feature_weights):
    tokens, heads, width = queries.shape
    groups = keys.shape[1]
    feats = feature_weights.shape[3]
    rows = width // (chips * subs)
    batch = 4
    batches = heads // batch
    vmem = pl.BlockSpec(memory_space=pltpu.VMEM)
    slot = pltpu.VMEM((heads, width + 8, feats), F32)
    pieces = (2, batches, chips, batch, rows, feats)
    query_grad, key_grad, value_grad, maps = pl.pallas_call(
        functools.partial(kernel, chips, subs, heads // groups, batch),
        out_shape=(
            jax.ShapeDtypeStruct((heads, tokens, width), BF16),
            jax.ShapeDtypeStruct((groups, tokens, width), BF16),
            jax.ShapeDtypeStruct((groups, tokens, width), BF16),
            jax.ShapeDtypeStruct((2, batches, batch, rows, feats), F32),
        ),
        in_specs=[vmem] * 5,
        out_specs=(vmem,) * 4,
        scratch_shapes=[
            pltpu.VMEM((heads, tokens, feats), BF16),
            pltpu.VMEM((heads, tokens, feats), BF16),
            pltpu.VMEM((heads, tokens, feats), F32),
            slot, slot, slot, slot,
            pltpu.VMEM((tokens, width), F32),
            pltpu.VMEM((groups, tokens, width), F32),
            pltpu.VMEM((2, batches, subs, chips, batch, rows, feats), F32),
            pltpu.VMEM(pieces, F32),
            pltpu.VMEM(pieces, F32),
            pltpu.VMEM((chips - 1, 2, batches, batch, rows, feats), F32),
        ]
        + [pltpu.SemaphoreType.DMA((heads,))] * 4
        + [pltpu.SemaphoreType.DMA((2, batches))] * 2
        + [pltpu.SemaphoreType.DMA((chips - 1, 2, batches))] * 2,
        compiler_params=pltpu.CompilerParams(
            collective_id=0, has_side_effects=True, vmem_limit_bytes=58 * 1024 * 1024
        ),
    )(
        queries.transpose(1, 0, 2),
        keys.transpose(1, 0, 2),
        values.transpose(1, 0, 2),
        out_grad.transpose(1, 0, 2),
        feature_weights,
    )
    return (
        query_grad.transpose(1, 0, 2),
        key_grad.transpose(1, 0, 2),
        value_grad.transpose(1, 0, 2),
        maps.reshape(2, heads, rows, feats).transpose(2, 0, 1, 3),
    )


def solution(mesh):
    chips = mesh.shape["seq"]
    subs = mesh.shape["sub"]
    rows = P(("grp", "seq", "sub"), "head", None)
    return jax.shard_map(
        functools.partial(shards, chips, subs),
        mesh=mesh,
        in_specs=(rows, rows, rows, rows, P(None, "head", None, None)),
        out_specs=(rows, rows, rows, P(("grp", "seq", "sub"), None, "head", None)),
        check_vma=False,
    )
```

time: 186 us -> 151 us (0.81)
  waiting for transfers between devices: 42.3 us -> 0 us
  Pallas kernels: 114 us -> 135 us
  between operations: 14 us -> 0.67 us
    reduce_scatter x1 -> x0, waiting for transfers between devices: 42.3 us -> none  [shards(): lax.psum_scatter(maps, ('seq', 'sub'), scatter_dimension=0, tiled=True)]
    pallas_call x1, Pallas kernels: 114 us -> 135 us  [shards(): pl.pallas_call(functools.partial(kernel, chips, subs, heads // groups, ba...]
    unnamed x10 -> x9, local copies, waits for them, and re-layouts: 8.06 us -> 6.17 us
  transfers between devices with their start and end apart: 1 -> 0, of which waited for: 1 -> 0; matrix products, arithmetic and copies ran while one was open for 2% -> 0% of each run, Pallas kernels for 0% -> 0%
where the time goes in v2:
time: 151 us
  Pallas kernels  135 us (89%)
  local copies, waits for them, and re-layouts  14.9 us (10%)
    pallas_call x1, Pallas kernels, shards(): pl.pallas_call(functools.partial(kernel, chips, subs, heads // groups, ba...  135 us
    unnamed x9, local copies, waits for them, and re-layouts  6.17 us
    transpose x1, local copies, waits for them, and re-layouts, shards(): out_grad.transpose(1, 0, 2)  5.87 us

profile of v2, /device:TPU:0, one launch (start us, length us, event | category | flops | bytes accessed | tf_op | source)
XLA Modules:
  0.0 150.6 jit_solution(8054165581354548557)
XLA Ops:
  0.6 1.9 %copy_bitcast_fusion.3 = (bf16[4,256,128]{2,1,0:T(8,128)(2,1)}, bf16[4,256,128]{2,1,0:T(8,128)(2,1)}) fusion(bf16[256,4,128]{2,1,0:T(4,128)(2,1)} %param.7, bf16[256,4,128]{2,1,0:T(4,128)(2,1)} %param.6), kind=kLoop, calls=%fused_computation.3 | loop fusion | bytes 1048576 | tf_op jit(solution)/shard_map/transpose | solution.py:337
  2.5 5.9 %copy_bitcast_fusion = (bf16[32,256,128]{2,1,0:T(8,128)(2,1)}, bf16[32,256,128]{2,1,0:T(8,128)(2,1)}) fusion(bf16[256,32,128]{2,1,0:T(8,128)(2,1)} %param.8, bf16[256,32,128]{2,1,0:T(8,128)(2,1)} %param.5), kind=kLoop, calls=%fused_computation | loop fusion | bytes 8388608 | tf_op jit(solution)/shard_map/transpose | solution.py:338
  8.4 135.1 %shard_map.84 = (bf16[32,256,128]{2,1,0:T(8,128)(2,1)}, bf16[4,256,128]{2,1,0:T(8,128)(2,1)}, bf16[4,256,128]{2,1,0:T(8,128)(2,1)}, f32[2,8,4,16,128]{4,3,2,1,0:T(8,128)}) custom-call(bf16[32,256,128]{2,1,0:T(8,128)(2,1)} %get-tuple-element.17.q_ref, bf16[4,256,128]{2,1,0:T(8,128)(2,1)} %get-tuple-element.19.k_ref, ...), custom_call_target="tpu_custom_call" | custom-call | tf_op jit(solution)/shard_map/pallas_call | solution.py:306
  143.5 0.0 copy-start.2
  143.5 0.0 copy-start.1
  143.5 0.0 copy-start
  143.5 4.3 %copy.14 = bf16[256,32,128]{2,1,0:T(8,128)(2,1)} copy(bf16[256,32,128]{2,0,1:T(8,128)(2,1)} %bitcast.15) | data formatting | bytes 4194304
  147.8 0.0 copy-done.2
  147.8 0.9 copy.15
  148.8 0.0 copy-done.1
  148.8 0.9 copy.16
  149.7 0.0 copy-done
  149.7 1.0 copy.22
Async XLA Ops:
  143.5 4.4 %copy-start.2 = (bf16[4,256,128]{2,1,0:T(8,128)(2,1)S(1)}, bf16[4,256,128]{2,1,0:T(8,128)(2,1)}, u32[]{:S(2)}) copy-start(bf16[4,256,128]{2,1,0:T(8,128)(2,1)} %get-tuple-element.9) | copy-start | bytes 786436
  143.5 5.3 %copy-start.1 = (bf16[4,256,128]{2,1,0:T(8,128)(2,1)S(1)}, bf16[4,256,128]{2,1,0:T(8,128)(2,1)}, u32[]{:S(2)}) copy-start(bf16[4,256,128]{2,1,0:T(8,128)(2,1)} %get-tuple-element.10) | copy-start | bytes 786436
  143.5 6.2 %copy-start = (f32[2,8,4,16,128]{4,3,2,1,0:T(8,128)S(1)}, f32[2,8,4,16,128]{4,3,2,1,0:T(8,128)}, u32[]{:S(2)}) copy-start(f32[2,8,4,16,128]{4,3,2,1,0:T(8,128)} %get-tuple-element.11) | copy-start | bytes 1572868

commit v3 on v2

v3 whole, which is shorter than its diff:
```python
import functools

import jax
import jax.numpy as jnp
from jax import lax
from jax.experimental import pallas as pl
from jax.experimental.pallas import tpu as pltpu
from jax.sharding import PartitionSpec as P

F32 = jnp.float32
BF16 = jnp.bfloat16
PAIR = 2


def dot(left, right, left_dim, right_dim):
    return lax.dot_general(
        left, right, (((left_dim,), (right_dim,)), ((), ())), preferred_element_type=F32
    )


def softmax(logits):
    grown = jnp.exp(logits - jnp.max(logits, axis=1, keepdims=True))
    return grown * (1.0 / jnp.sum(grown, axis=1, keepdims=True))


def logit_grad(low, grad):
    feat = low.astype(F32)
    return (feat * (grad - jnp.sum(feat * grad, axis=1, keepdims=True))).astype(BF16)


def kernel(
    chips, subs, group_size, batch,
    q_ref, k_ref, v_ref, og_ref, w_ref,
    qg_ref, kg_ref, vg_ref, mg_ref,
    ql_ref, kl_ref, kf_ref,
    fwd_in, fwd_out, bwd_in, bwd_out, k_acc, v_acc,
    map_own, map_got, map_sum, map_far,
    fwd_send, fwd_recv, bwd_send, bwd_recv,
    pair_send, pair_recv, far_send, far_recv,
):
    heads, tokens, width = q_ref.shape
    feats = w_ref.shape[3]
    blocks = chips * subs
    chip = lax.axis_index("seq")
    core = lax.axis_index("sub")
    me = chip * subs + core
    before = jnp.maximum(me - 1, 0)
    after = jnp.minimum(me + 1, blocks - 1)
    batches = heads // batch

    def place(block):
        return {"seq": block // subs, "sub": block % subs}

    def send(src, dst, send_sem, recv_sem, target):
        return pltpu.make_async_remote_copy(
            src_ref=src, dst_ref=dst, send_sem=send_sem, recv_sem=recv_sem,
            device_id=target, device_id_type=pl.DeviceIdType.MESH,
        )

    def pair(p):
        return pl.ds(p * PAIR, PAIR)

    def fwd_copy(h):
        return send(
            fwd_out.at[pair(h)], fwd_in.at[pair(h)], fwd_send.at[h], fwd_recv.at[h], place(after)
        )

    def bwd_copy(h):
        return send(
            bwd_out.at[pair(h)], bwd_in.at[pair(h)], bwd_send.at[h], bwd_recv.at[h], place(before)
        )

    def pair_copy(side, n):
        return send(
            map_own.at[side, n, 1 - core], map_got.at[side, n],
            pair_send.at[side, n], pair_recv.at[side, n],
            {"seq": chip, "sub": 1 - core},
        )

    def far_copy(side, n, hop):
        to = (chip + hop) % chips
        return send(
            map_sum.at[side, n, to], map_far.at[hop - 1, side, n],
            far_send.at[hop - 1, side, n], far_recv.at[hop - 1, side, n],
            {"seq": to, "sub": core},
        )

    barrier = pltpu.get_barrier_semaphore()
    for step in range(1, blocks):
        pl.semaphore_signal(
            barrier, inc=1, device_id=place((me + step) % blocks),
            device_id_type=pl.DeviceIdType.MESH,
        )
    pl.semaphore_wait(barrier, blocks - 1)

    @pl.when(me == 0)
    def _():
        fwd_in[...] = jnp.zeros_like(fwd_in)

    @pl.when(me == blocks - 1)
    def _():
        bwd_in[...] = jnp.zeros_like(bwd_in)

    pairs = heads // PAIR
    turns = batch // PAIR
    fwd_lag = jnp.minimum(me, pairs // 2)
    bwd_lag = jnp.minimum(blocks - 1 - me, pairs // 2)
    k_acc[...] = jnp.zeros_like(k_acc)
    v_acc[...] = jnp.zeros_like(v_acc)

    def fwd_step(h):
        @pl.when(me > 0)
        def _():
            fwd_copy(h).wait_recv()

        @pl.when(me < blocks - 1)
        def _():
            fwd_out[pair(h)] += fwd_in[pair(h)]
            fwd_copy(h).start()

    def bwd_step(h):
        @pl.when(me < blocks - 1)
        def _():
            bwd_copy(h).wait_recv()

        @pl.when(me > 0)
        def _():
            bwd_out[pair(h)] += bwd_in[pair(h)]
            bwd_copy(h).start()

    def put_map(side, h, product):
        rows = product.reshape(chips, subs, width // blocks, feats)
        for c in range(subs):
            map_own[side, h // batch, c, :, h % batch] = rows[:, c]

    def spread_map(side, n):
        pair_copy(side, n).wait_recv()
        map_sum[side, n] = map_own[side, n, core] + map_got[side, n]
        for hop in range(1, chips):
            far_copy(side, n, hop).start()

    def send_map(side, p):
        @pl.when(p % turns == turns - 1)
        def _():
            pair_copy(side, p // turns).start()

        @pl.when(jnp.logical_and(p % turns == 0, p >= turns))
        def _():
            spread_map(side, p // turns - 1)

    def halves(both):
        return [both[:, u * feats:(u + 1) * feats] for u in range(PAIR)]

    def side_by_side(parts):
        return jnp.concatenate(parts, axis=1)

    def features(p, carry):
        heads_now = [p * PAIR + u for u in range(PAIR)]
        g = p * PAIR // group_size
        queries_low = [
            softmax(dot(q_ref[h], w_ref[0, h], 1, 0)).astype(BF16) for h in heads_now
        ]
        logits = dot(k_ref[g], side_by_side([w_ref[1, h] for h in heads_now]), 1, 0)
        keys_low = [softmax(part).astype(BF16) for part in halves(logits)]
        own = halves(dot(v_ref[g], side_by_side(keys_low), 0, 0))
        for u, h in enumerate(heads_now):
            ql_ref[h] = queries_low[u]
            kl_ref[h] = keys_low[u]
            fwd_out[h, 0:width] = own[u]
            fwd_out[h, width:width + 8] = jnp.broadcast_to(
                jnp.sum(keys_low[u].astype(F32), axis=0, keepdims=True), (8, feats)
            )

        @pl.when(p >= fwd_lag)
        def _():
            fwd_step(p - fwd_lag)

        return carry

    lax.fori_loop(0, pairs, features, 0)

    def causal():
        rows = lax.broadcasted_iota(jnp.int32, (tokens, tokens), 0)
        return rows >= lax.broadcasted_iota(jnp.int32, (tokens, tokens), 1)

    def queries_side(p, carry):
        @pl.when(p < fwd_lag)
        def _():
            fwd_step(pairs - fwd_lag + p)

        heads_now = [p * PAIR + u for u in range(PAIR)]
        g = p * PAIR // group_size
        value_rows = v_ref[g]
        below = causal()
        done = []
        for h in heads_now:
            query_low = ql_ref[h]
            key_low = kl_ref[h]
            state = fwd_in[h, 0:width].astype(BF16)
            state_z = fwd_in[h, width:width + 1]
            masked = jnp.where(below, dot(query_low, key_low, 1, 1), 0.0)
            weights = masked.astype(BF16)
            numerator = dot(weights, value_rows, 1, 0) + dot(query_low, state, 1, 1)
            query_round = query_low.astype(F32)
            denominator = jnp.sum(masked, axis=1, keepdims=True) + jnp.sum(
                query_round * state_z, axis=1, keepdims=True
            )
            grad = og_ref[h].astype(F32)
            numer_grad = (grad * (1.0 / denominator)).astype(BF16)
            denom_grad = -jnp.sum(grad * numerator, axis=1, keepdims=True) / (
                denominator * denominator
            )
            own = dot(numer_grad, query_low, 0, 0)
            own_z = jnp.sum(query_round * denom_grad, axis=0, keepdims=True)
            score_grad = jnp.where(
                below, dot(numer_grad, value_rows, 1, 1) + denom_grad, 0.0
            ).astype(BF16)
            query_feat_grad = (
                dot(score_grad, key_low, 1, 0)
                + dot(numer_grad, state, 1, 0)
                + denom_grad * state_z
            )
            query_logit_grad = logit_grad(query_low, query_feat_grad)
            query_grad = dot(query_logit_grad, w_ref[0, h], 1, 1).astype(BF16)
            map_term = dot(q_ref[h], query_logit_grad, 0, 0)
            key_term = dot(score_grad, query_low, 0, 0)
            done.append(
                (own, own_z, query_grad, map_term, key_term, weights, numer_grad)
            )
        value_term = dot(
            jnp.concatenate([item[5] for item in done], axis=0),
            jnp.concatenate([item[6] for item in done], axis=0), 0, 0,
        )
        for h, item in zip(heads_now, done):
            bwd_out[h, 0:width] = item[0]
            bwd_out[h, width:width + 8] = jnp.broadcast_to(item[1], (8, feats))
            qg_ref[h] = item[2]
            put_map(0, h, item[3])
            kf_ref[h] = item[4]
        v_acc[g] += value_term

        @pl.when(p >= bwd_lag)
        def _():
            bwd_step(p - bwd_lag)

        send_map(0, p)
        return carry

    lax.fori_loop(0, pairs, queries_side, 0)

    def keys_side(p, carry):
        @pl.when(p < bwd_lag)
        def _():
            bwd_step(pairs - bwd_lag + p)

        @pl.when(p == 0)
        def _():
            spread_map(0, batches - 1)

        heads_now = [p * PAIR + u for u in range(PAIR)]
        g = p * PAIR // group_size
        keys_low = [kl_ref[h] for h in heads_now]
        back = side_by_side([bwd_in[h, 0:width].astype(BF16) for h in heads_now])
        far = halves(dot(v_ref[g], back, 1, 0))
        logit_grads = side_by_side([
            logit_grad(keys_low[u], kf_ref[h] + far[u] + bwd_in[h, width:width + 1])
            for u, h in enumerate(heads_now)
        ])
        maps = halves(dot(k_ref[g], logit_grads, 0, 0))
        key_term = dot(
            logit_grads, side_by_side([w_ref[1, h] for h in heads_now]), 1, 1
        )
        value_term = dot(side_by_side(keys_low), back, 1, 1)
        for u, h in enumerate(heads_now):
            put_map(1, h, maps[u])
        k_acc[g] += key_term
        v_acc[g] += value_term
        send_map(1, p)
        return carry

    lax.fori_loop(0, pairs, keys_side, 0)
    spread_map(1, batches - 1)
    kg_ref[...] = k_acc[...].astype(BF16)
    vg_ref[...] = v_acc[...].astype(BF16)

    for side in range(2):
        def finish(n, carry):
            total = map_sum[side, n, chip]
            for hop in range(1, chips):
                far_copy(side, n, hop).wait_recv()
                total += map_far[hop - 1, side, n]
            mg_ref[side, n] = total
            pair_copy(side, n).wait_send()
            for hop in range(1, chips):
                far_copy(side, n, hop).wait_send()
            return carry

        lax.fori_loop(0, batches, finish, 0)

    def drain(h, carry):
        @pl.when(me < blocks - 1)
        def _():
            fwd_copy(h).wait_send()

        @pl.when(me > 0)
        def _():
            bwd_copy(h).wait_send()

        return carry

    lax.fori_loop(0, pairs, drain, 0)


def shards(chips, subs, queries, keys, values, out_grad, feature_weights):
    tokens, heads, width = queries.shape
    groups = keys.shape[1]
    feats = feature_weights.shape[3]
    rows = width // (chips * subs)
    batch = 4
    batches = heads // batch
    vmem = pl.BlockSpec(memory_space=pltpu.VMEM)
    slot = pltpu.VMEM((heads, width + 8, feats), F32)
    pieces = (2, batches, chips, batch, rows, feats)
    query_grad, key_grad, value_grad, maps = pl.pallas_call(
        functools.partial(kernel, chips, subs, heads // groups, batch),
        out_shape=(
            jax.ShapeDtypeStruct((heads, tokens, width), BF16),
            jax.ShapeDtypeStruct((groups, tokens, width), BF16),
            jax.ShapeDtypeStruct((groups, tokens, width), BF16),
            jax.ShapeDtypeStruct((2, batches, batch, rows, feats), F32),
        ),
        in_specs=[vmem] * 5,
        out_specs=(vmem,) * 4,
        scratch_shapes=[
            pltpu.VMEM((heads, tokens, feats), BF16),
            pltpu.VMEM((heads, tokens, feats), BF16),
            pltpu.VMEM((heads, tokens, feats), F32),
            slot, slot, slot, slot,
            pltpu.VMEM((groups, tokens, width), F32),
            pltpu.VMEM((groups, tokens, width), F32),
            pltpu.VMEM((2, batches, subs, chips, batch, rows, feats), F32),
            pltpu.VMEM(pieces, F32),
            pltpu.VMEM(pieces, F32),
            pltpu.VMEM((chips - 1, 2, batches, batch, rows, feats), F32),
        ]
        + [pltpu.SemaphoreType.DMA((heads // PAIR,))] * 4
        + [pltpu.SemaphoreType.DMA((2, batches))] * 2
        + [pltpu.SemaphoreType.DMA((chips - 1, 2, batches))] * 2,
        compiler_params=pltpu.CompilerParams(
            collective_id=0, has_side_effects=True, vmem_limit_bytes=58 * 1024 * 1024
        ),
    )(
        queries.transpose(1, 0, 2),
        keys.transpose(1, 0, 2),
        values.transpose(1, 0, 2),
        out_grad.transpose(1, 0, 2),
        feature_weights,
    )
    return (
        query_grad.transpose(1, 0, 2),
        key_grad.transpose(1, 0, 2),
        value_grad.transpose(1, 0, 2),
        maps.reshape(2, heads, rows, feats).transpose(2, 0, 1, 3),
    )


def solution(mesh):
    chips = mesh.shape["seq"]
    subs = mesh.shape["sub"]
    rows = P(("grp", "seq", "sub"), "head", None)
    return jax.shard_map(
        functools.partial(shards, chips, subs),
        mesh=mesh,
        in_specs=(rows, rows, rows, rows, P(None, "head", None, None)),
        out_specs=(rows, rows, rows, P(("grp", "seq", "sub"), None, "head", None)),
        check_vma=False,
    )
```

time: 151 us -> 154 us (1.020)
  Pallas kernels: 135 us -> 138 us
    pallas_call x1, Pallas kernels: 135 us -> 138 us  [shards(): pl.pallas_call(functools.partial(kernel, chips, subs, heads // groups, ba...]
where the time goes in v3:
time: 154 us
  Pallas kernels  138 us (90%)
  local copies, waits for them, and re-layouts  14.9 us (10%)
    pallas_call x1, Pallas kernels, shards(): pl.pallas_call(functools.partial(kernel, chips, subs, heads // groups, ba...  138 us
    unnamed x9, local copies, waits for them, and re-layouts  6.17 us
    transpose x1, local copies, waits for them, and re-layouts, shards(): out_grad.transpose(1, 0, 2)  5.87 us

profile of v3, /device:TPU:0, one launch (start us, length us, event | category | flops | bytes accessed | tf_op | source)
XLA Modules:
  0.0 153.8 jit_solution(5508153322786347647)
XLA Ops:
  0.6 1.9 %copy_bitcast_fusion.3 = (bf16[4,256,128]{2,1,0:T(8,128)(2,1)}, bf16[4,256,128]{2,1,0:T(8,128)(2,1)}) fusion(bf16[256,4,128]{2,1,0:T(4,128)(2,1)} %param.7, bf16[256,4,128]{2,1,0:T(4,128)(2,1)} %param.6), kind=kLoop, calls=%fused_computation.3 | loop fusion | bytes 1048576 | tf_op jit(solution)/shard_map/transpose | solution.py:355
  2.5 5.9 %copy_bitcast_fusion = (bf16[32,256,128]{2,1,0:T(8,128)(2,1)}, bf16[32,256,128]{2,1,0:T(8,128)(2,1)}) fusion(bf16[256,32,128]{2,1,0:T(8,128)(2,1)} %param.8, bf16[256,32,128]{2,1,0:T(8,128)(2,1)} %param.5), kind=kLoop, calls=%fused_computation | loop fusion | bytes 8388608 | tf_op jit(solution)/shard_map/transpose | solution.py:356
  8.4 138.3 %shard_map.84 = (bf16[32,256,128]{2,1,0:T(8,128)(2,1)}, bf16[4,256,128]{2,1,0:T(8,128)(2,1)}, bf16[4,256,128]{2,1,0:T(8,128)(2,1)}, f32[2,8,4,16,128]{4,3,2,1,0:T(8,128)}) custom-call(bf16[32,256,128]{2,1,0:T(8,128)(2,1)} %get-tuple-element.17.q_ref, bf16[4,256,128]{2,1,0:T(8,128)(2,1)} %get-tuple-element.19.k_ref, ...), custom_call_target="tpu_custom_call" | custom-call | tf_op jit(solution)/shard_map/pallas_call | solution.py:324
  146.7 0.0 copy-start.2
  146.7 0.0 copy-start.1
  146.7 0.0 copy-start
  146.7 4.3 %copy.14 = bf16[256,32,128]{2,1,0:T(8,128)(2,1)} copy(bf16[256,32,128]{2,0,1:T(8,128)(2,1)} %bitcast.15) | data formatting | bytes 4194304
  151.0 0.0 copy-done.2
  151.0 0.9 copy.15
  151.9 0.0 copy-done.1
  152.0 0.9 copy.16
  152.9 0.0 copy-done
  152.9 1.0 copy.22
Async XLA Ops:
  146.7 4.4 %copy-start.2 = (bf16[4,256,128]{2,1,0:T(8,128)(2,1)S(1)}, bf16[4,256,128]{2,1,0:T(8,128)(2,1)}, u32[]{:S(2)}) copy-start(bf16[4,256,128]{2,1,0:T(8,128)(2,1)} %get-tuple-element.9) | copy-start | bytes 786436
  146.7 5.3 %copy-start.1 = (bf16[4,256,128]{2,1,0:T(8,128)(2,1)S(1)}, bf16[4,256,128]{2,1,0:T(8,128)(2,1)}, u32[]{:S(2)}) copy-start(bf16[4,256,128]{2,1,0:T(8,128)(2,1)} %get-tuple-element.10) | copy-start | bytes 786436
  146.7 6.2 %copy-start = (f32[2,8,4,16,128]{4,3,2,1,0:T(8,128)S(1)}, f32[2,8,4,16,128]{4,3,2,1,0:T(8,128)}, u32[]{:S(2)}) copy-start(f32[2,8,4,16,128]{4,3,2,1,0:T(8,128)} %get-tuple-element.11) | copy-start | bytes 1572868

commit v4 on v2

--- a/solution.py
+++ b/solution.py
@@ -9,7 +9,7 @@
 
 F32 = jnp.float32
 BF16 = jnp.bfloat16
-LAG = 2
+LAG = 1
 
 
 def dot(left, right, left_dim, right_dim):

time: 151 us -> 162 us (1.073)
  Pallas kernels: 135 us -> 146 us
    pallas_call x1, Pallas kernels: 135 us -> 146 us  [shards(): pl.pallas_call(functools.partial(kernel, chips, subs, heads // groups, ba...]
where the time goes in v4:
time: 162 us
  Pallas kernels  146 us (90%)
  local copies, waits for them, and re-layouts  14.9 us (9%)
    pallas_call x1, Pallas kernels, shards(): pl.pallas_call(functools.partial(kernel, chips, subs, heads // groups, ba...  146 us
    unnamed x9, local copies, waits for them, and re-layouts  6.17 us
    transpose x1, local copies, waits for them, and re-layouts, shards(): out_grad.transpose(1, 0, 2)  5.87 us

profile of v4, /device:TPU:0, one launch (start us, length us, event | category | flops | bytes accessed | tf_op | source)
XLA Modules:
  0.0 161.8 jit_solution(18274551954234158974)
XLA Ops:
  0.6 1.9 %copy_bitcast_fusion.3 = (bf16[4,256,128]{2,1,0:T(8,128)(2,1)}, bf16[4,256,128]{2,1,0:T(8,128)(2,1)}) fusion(bf16[256,4,128]{2,1,0:T(4,128)(2,1)} %param.7, bf16[256,4,128]{2,1,0:T(4,128)(2,1)} %param.6), kind=kLoop, calls=%fused_computation.3 | loop fusion | bytes 1048576 | tf_op jit(solution)/shard_map/transpose | solution.py:337
  2.5 5.9 %copy_bitcast_fusion = (bf16[32,256,128]{2,1,0:T(8,128)(2,1)}, bf16[32,256,128]{2,1,0:T(8,128)(2,1)}) fusion(bf16[256,32,128]{2,1,0:T(8,128)(2,1)} %param.8, bf16[256,32,128]{2,1,0:T(8,128)(2,1)} %param.5), kind=kLoop, calls=%fused_computation | loop fusion | bytes 8388608 | tf_op jit(solution)/shard_map/transpose | solution.py:338
  8.4 146.2 %shard_map.84 = (bf16[32,256,128]{2,1,0:T(8,128)(2,1)}, bf16[4,256,128]{2,1,0:T(8,128)(2,1)}, bf16[4,256,128]{2,1,0:T(8,128)(2,1)}, f32[2,8,4,16,128]{4,3,2,1,0:T(8,128)}) custom-call(bf16[32,256,128]{2,1,0:T(8,128)(2,1)} %get-tuple-element.17.q_ref, bf16[4,256,128]{2,1,0:T(8,128)(2,1)} %get-tuple-element.19.k_ref, ...), custom_call_target="tpu_custom_call" | custom-call | tf_op jit(solution)/shard_map/pallas_call | solution.py:306
  154.6 0.0 copy-start.2
  154.6 0.0 copy-start.1
  154.6 0.0 copy-start
  154.6 4.3 %copy.14 = bf16[256,32,128]{2,1,0:T(8,128)(2,1)} copy(bf16[256,32,128]{2,0,1:T(8,128)(2,1)} %bitcast.15) | data formatting | bytes 4194304
  159.0 0.0 copy-done.2
  159.0 0.9 copy.15
  159.9 0.0 copy-done.1
  159.9 0.9 copy.16
  160.8 0.0 copy-done
  160.8 1.0 copy.22
Async XLA Ops:
  154.6 4.4 %copy-start.2 = (bf16[4,256,128]{2,1,0:T(8,128)(2,1)S(1)}, bf16[4,256,128]{2,1,0:T(8,128)(2,1)}, u32[]{:S(2)}) copy-start(bf16[4,256,128]{2,1,0:T(8,128)(2,1)} %get-tuple-element.9) | copy-start | bytes 786436
  154.6 5.3 %copy-start.1 = (bf16[4,256,128]{2,1,0:T(8,128)(2,1)S(1)}, bf16[4,256,128]{2,1,0:T(8,128)(2,1)}, u32[]{:S(2)}) copy-start(bf16[4,256,128]{2,1,0:T(8,128)(2,1)} %get-tuple-element.10) | copy-start | bytes 786436
  154.6 6.2 %copy-start = (f32[2,8,4,16,128]{4,3,2,1,0:T(8,128)S(1)}, f32[2,8,4,16,128]{4,3,2,1,0:T(8,128)}, u32[]{:S(2)}) copy-start(f32[2,8,4,16,128]{4,3,2,1,0:T(8,128)} %get-tuple-element.11) | copy-start | bytes 1572868

commit v5 on v4

--- a/solution.py
+++ b/solution.py
@@ -9,7 +9,7 @@
 
 F32 = jnp.float32
 BF16 = jnp.bfloat16
-LAG = 1
+LAG = 3
 
 
 def dot(left, right, left_dim, right_dim):

time: 162 us -> 149 us (0.920)
  Pallas kernels: 146 us -> 133 us
    pallas_call x1, Pallas kernels: 146 us -> 133 us  [shards(): pl.pallas_call(functools.partial(kernel, chips, subs, heads // groups, ba...]
where the time goes in v5:
time: 149 us
  Pallas kernels  133 us (89%)
  local copies, waits for them, and re-layouts  14.9 us (10%)
    pallas_call x1, Pallas kernels, shards(): pl.pallas_call(functools.partial(kernel, chips, subs, heads // groups, ba...  133 us
    unnamed x9, local copies, waits for them, and re-layouts  6.17 us
    transpose x1, local copies, waits for them, and re-layouts, shards(): out_grad.transpose(1, 0, 2)  5.87 us

profile of v5, /device:TPU:0, one launch (start us, length us, event | category | flops | bytes accessed | tf_op | source)
XLA Modules:
  0.0 148.7 jit_solution(2955707590623306240)
XLA Ops:
  0.6 1.9 %copy_bitcast_fusion.3 = (bf16[4,256,128]{2,1,0:T(8,128)(2,1)}, bf16[4,256,128]{2,1,0:T(8,128)(2,1)}) fusion(bf16[256,4,128]{2,1,0:T(4,128)(2,1)} %param.7, bf16[256,4,128]{2,1,0:T(4,128)(2,1)} %param.6), kind=kLoop, calls=%fused_computation.3 | loop fusion | bytes 1048576 | tf_op jit(solution)/shard_map/transpose | solution.py:337
  2.5 5.9 %copy_bitcast_fusion = (bf16[32,256,128]{2,1,0:T(8,128)(2,1)}, bf16[32,256,128]{2,1,0:T(8,128)(2,1)}) fusion(bf16[256,32,128]{2,1,0:T(8,128)(2,1)} %param.8, bf16[256,32,128]{2,1,0:T(8,128)(2,1)} %param.5), kind=kLoop, calls=%fused_computation | loop fusion | bytes 8388608 | tf_op jit(solution)/shard_map/transpose | solution.py:338
  8.4 133.1 %shard_map.84 = (bf16[32,256,128]{2,1,0:T(8,128)(2,1)}, bf16[4,256,128]{2,1,0:T(8,128)(2,1)}, bf16[4,256,128]{2,1,0:T(8,128)(2,1)}, f32[2,8,4,16,128]{4,3,2,1,0:T(8,128)}) custom-call(bf16[32,256,128]{2,1,0:T(8,128)(2,1)} %get-tuple-element.17.q_ref, bf16[4,256,128]{2,1,0:T(8,128)(2,1)} %get-tuple-element.19.k_ref, ...), custom_call_target="tpu_custom_call" | custom-call | tf_op jit(solution)/shard_map/pallas_call | solution.py:306
  141.5 0.0 copy-start.2
  141.5 0.0 copy-start.1
  141.5 0.0 copy-start
  141.5 4.3 %copy.14 = bf16[256,32,128]{2,1,0:T(8,128)(2,1)} copy(bf16[256,32,128]{2,0,1:T(8,128)(2,1)} %bitcast.15) | data formatting | bytes 4194304
  145.9 0.0 copy-done.2
  145.9 0.9 copy.15
  146.8 0.0 copy-done.1
  146.8 0.9 copy.16
  147.7 0.0 copy-done
  147.7 1.0 copy.22
Async XLA Ops:
  141.5 4.4 %copy-start.2 = (bf16[4,256,128]{2,1,0:T(8,128)(2,1)S(1)}, bf16[4,256,128]{2,1,0:T(8,128)(2,1)}, u32[]{:S(2)}) copy-start(bf16[4,256,128]{2,1,0:T(8,128)(2,1)} %get-tuple-element.9) | copy-start | bytes 786436
  141.5 5.3 %copy-start.1 = (bf16[4,256,128]{2,1,0:T(8,128)(2,1)S(1)}, bf16[4,256,128]{2,1,0:T(8,128)(2,1)}, u32[]{:S(2)}) copy-start(bf16[4,256,128]{2,1,0:T(8,128)(2,1)} %get-tuple-element.10) | copy-start | bytes 786436
  141.5 6.2 %copy-start = (f32[2,8,4,16,128]{4,3,2,1,0:T(8,128)S(1)}, f32[2,8,4,16,128]{4,3,2,1,0:T(8,128)}, u32[]{:S(2)}) copy-start(f32[2,8,4,16,128]{4,3,2,1,0:T(8,128)} %get-tuple-element.11) | copy-start | bytes 1572868
